TPU v7x, 32 devices: a whole 2x2x4 slice. The times are simulated.
32 devices in a mesh: grp: 4 (over x, core), wav: 8 (over z, y).
Axes of the slice: x: 2, y: 2, z: 4, core: 2. Of those that a mesh axis runs over, the one named last changes fastest.
Arguments:
- spectra: float32 [3, 8, 16, 2, 2560], P(None, 'grp', 'wav'), may hold values from -6 to 6
- legendre: float32 [16, 2560, 32], P('wav'), may hold values from -0.03125 to 0.03125
- wave_number: int32 [16], replicated, may hold values from 0 to 2559, as said below
- cycle_points: int32 [32], replicated, may hold values from 20 to 10256, as said below
- cycle_owner: int32 [64], replicated, may hold values from 0 to 63, each once
Outputs:
- grid_columns: float32 [64, 3, 8, 11264], P('grp', None, None, 'wav')
Inputs may be any that keep to these rules, and one draw needn't show every extreme that they name: `wave_number`: all distinct; entries 2 i and 2 i + 1 sum to 2559. `cycle_points`: each is 20 + 4 k for a whole k, rising with the latitude index; 20 and 10256 both occur. `cycle_owner`: A permutation of the cycles: 0 to 31 northern, 32 + i the southern mirror of latitude i.
All inputs are finite; a program needn't handle non-finite values.
Results may differ from a plain program's by a relative error of at most 0.0003.
Values sent between devices are 32-bit elements; how exact they have to be, the bound alone decides.
A program may use at most 128 MiB of HBM per device.

v0:
```python
import jax
import jax.numpy as jnp
from jax import lax
from jax.sharding import PartitionSpec as P

RMAX = 10256


TWO_PI = 6.283185307179586
HIGHEST = lax.Precision.HIGHEST


def synthesis(coeffs, wave_list, lengths, points_count):
    points = jnp.arange(points_count, dtype=jnp.int32)
    weight = jnp.where(wave_list == 0, 1.0, 2.0).astype(jnp.float32)
    wave_total = wave_list.shape[0]

    def one_cycle(cycle_args):
        cycle_block, cycle_length = cycle_args
        phases = wave_list[:, None] * points[None, :] % cycle_length
        angles = phases.astype(jnp.float32) * (TWO_PI / cycle_length.astype(jnp.float32))
        cosine = weight[:, None] * jnp.cos(angles)
        sine_part = -weight[:, None] * jnp.sin(angles)
        fourier_basis = jnp.stack([cosine, sine_part], axis=1).reshape(2 * wave_total, points_count)
        flattened = cycle_block.reshape(-1, 2 * wave_total)
        values = jnp.dot(
            flattened, fourier_basis, precision=HIGHEST, preferred_element_type=jnp.float32
        )
        values = jnp.where(points[None, :] < cycle_length, values, 0.0)
        return values.reshape(cycle_block.shape[:-1] + (points_count,))

    return lax.map(one_cycle, (coeffs, lengths))


def body(spectra, legendre, wave_number, cycle_points, cycle_owner):
    column = lax.axis_index("wav")
    wav_size = lax.axis_size("wav")
    wave_local = legendre.shape[0]
    degree_rows = legendre.shape[1]
    my_waves = lax.dynamic_slice_in_dim(wave_number, column * wave_local, wave_local)
    offsets = jnp.arange(degree_rows, dtype=jnp.int32)
    inside = my_waves[:, None] + offsets[None, :] < degree_rows
    masked = jnp.where(inside[None, None, :, None, :], spectra, 0.0)
    parity_signs = jnp.where(offsets % 2 == 0, 1.0, -1.0).astype(jnp.float32)
    mirrored = jnp.concatenate([legendre, legendre * parity_signs[None, :, None]], axis=2)
    fourier = jnp.einsum("flmck,mki->iflmc", masked, mirrored, precision=HIGHEST)
    placed = jnp.take(fourier, cycle_owner, axis=0)
    cycle_total = placed.shape[0]
    rows_first = placed.reshape(cycle_total, 3, placed.shape[2], 2 * wave_local)
    cycle_lengths = jnp.concatenate([cycle_points, cycle_points])[cycle_owner]
    segment = (RMAX + 128 * wav_size - 1) // (128 * wav_size) * 128
    owned_cycles = cycle_total // wav_size
    my_lengths = lax.dynamic_slice_in_dim(cycle_lengths, column * owned_cycles, owned_cycles)
    grid_rows = synthesis(
        lax.all_to_all(rows_first, "wav", split_axis=0, concat_axis=3, tiled=True),
        wave_number,
        my_lengths,
        segment * wav_size,
    )
    return lax.all_to_all(
        lax.all_to_all(grid_rows, "wav", split_axis=3, concat_axis=0, tiled=True),
        "grp",
        split_axis=0,
        concat_axis=2,
        tiled=True,
    )


def solution(mesh):
    in_specs = (P(None, "grp", "wav", None, None), P("wav", None, None), P(), P(), P())
    out_specs = P("grp", None, None, "wav")
    return jax.shard_map(body, mesh=mesh, in_specs=in_specs, out_specs=out_specs, check_vma=False)
```

profile of v0, /device:TPU:0, one launch (start us, length us, event | category | flops | bytes accessed | tf_op | source)
XLA Modules:
  0.0 470.3 jit_solution(11848832850669531149)
XLA Ops:
  2.2 1.1 broadcast_select_fusion
  3.3 1.1 broadcast_multiply_fusion
  4.4 2.4 fusion.16
  9.2 7.3 %all-to-all-start = ((f32[8,1,192]{2,1,0:T(1,128)}), f32[8,1,192]{2,1,0:T(1,128)S(1)}, u32[]{:S(2)}, u32[]{:S(2)}) async-start(f32[8,1,192]{2,1,0:T(1,128)} %reshape.234), calls=%async_computation | async-start | bytes 16384 | tf_op jit(solution)/shard_map/all_to_all | solution.py:55
  17.4 5.6 %all-to-all-done = f32[8,1,192]{2,1,0:T(1,128)S(1)} async-done(((f32[8,1,192]{2,1,0:T(1,128)}), f32[8,1,192]{2,1,0:T(1,128)S(1)}, u32[]{:S(2)}, u32[]{:S(2)}) %all-to-all-start) | async-done | bytes 6176 | tf_op jit(solution)/shard_map/all_to_all | solution.py:55
  25.0 134.5 %while.13 = (s32[]{:T(128)}, f32[8,3,2,11264]{3,2,1,0:T(2,128)}, s32[8]{0:T(128)S(1)}, f32[8,3,2,32]{3,2,1,0:T(2,128)S(1)}, f32[16]{0:T(128)S(1)}, /*index=5*/s3...) while((s32[]{:T(128)}, f32[8,3,2,11264]{3,2,1,0:T(2,128)}, ...), condition=%wide.region_1.2_spmd.clone.clone, body=%wide.region_0.1_spmd.clone.clone.sunk | while | flops 28554248 | bytes 12912769 | solution.py:32
  28.4 9.6 %fusion.31 = (f32[16,1,11264]{2,0,1:T(8,128)S(1)}, f32[16,1,11264]{2,0,1:T(8,128)S(1)}) fusion(f32[]{:T(128)S(6)} %div.7, s32[]{:T(128)S(6)} %select_n.118, s32[16]{0:T(128)S(1)} %get-tuple-element.247, f32[16]{0:T(128)S(1)} %get-tuple-element.246, pred[]{:T(512)S(6)} %lt.122, f32[16]{0:T(128)S(1)} %bitcast.47), kind=kLoop, calls=%fused_computation.14.clone.1 | loop fusion | flops 2162688 | bytes 1441993 | tf_op jit(solution)/shard_map/while/body/eval_jaxpr/mul | solution.py:22
  38.1 1.1 copy.85
  39.2 1.0 reshape.241
  45.2 9.6 %fusion.31 = (f32[16,1,11264]{2,0,1:T(8,128)S(1)}, f32[16,1,11264]{2,0,1:T(8,128)S(1)}) fusion(f32[]{:T(128)S(6)} %div.7, s32[]{:T(128)S(6)} %select_n.118, s32[16]{0:T(128)S(1)} %get-tuple-element.247, f32[16]{0:T(128)S(1)} %get-tuple-element.246, pred[]{:T(512)S(6)} %lt.122, f32[16]{0:T(128)S(1)} %bitcast.47), kind=kLoop, calls=%fused_computation.14.clone.1 | loop fusion | flops 2162688 | bytes 1441993 | tf_op jit(solution)/shard_map/while/body/eval_jaxpr/mul | solution.py:22
  54.8 1.1 copy.85
  61.9 9.6 %fusion.31 = (f32[16,1,11264]{2,0,1:T(8,128)S(1)}, f32[16,1,11264]{2,0,1:T(8,128)S(1)}) fusion(f32[]{:T(128)S(6)} %div.7, s32[]{:T(128)S(6)} %select_n.118, s32[16]{0:T(128)S(1)} %get-tuple-element.247, f32[16]{0:T(128)S(1)} %get-tuple-element.246, pred[]{:T(512)S(6)} %lt.122, f32[16]{0:T(128)S(1)} %bitcast.47), kind=kLoop, calls=%fused_computation.14.clone.1 | loop fusion | flops 2162688 | bytes 1441993 | tf_op jit(solution)/shard_map/while/body/eval_jaxpr/mul | solution.py:22
  71.6 1.1 copy.85
  78.6 9.6 %fusion.31 = (f32[16,1,11264]{2,0,1:T(8,128)S(1)}, f32[16,1,11264]{2,0,1:T(8,128)S(1)}) fusion(f32[]{:T(128)S(6)} %div.7, s32[]{:T(128)S(6)} %select_n.118, s32[16]{0:T(128)S(1)} %get-tuple-element.247, f32[16]{0:T(128)S(1)} %get-tuple-element.246, pred[]{:T(512)S(6)} %lt.122, f32[16]{0:T(128)S(1)} %bitcast.47), kind=kLoop, calls=%fused_computation.14.clone.1 | loop fusion | flops 2162688 | bytes 1441993 | tf_op jit(solution)/shard_map/while/body/eval_jaxpr/mul | solution.py:22
  88.3 1.1 copy.85
  95.4 9.6 %fusion.31 = (f32[16,1,11264]{2,0,1:T(8,128)S(1)}, f32[16,1,11264]{2,0,1:T(8,128)S(1)}) fusion(f32[]{:T(128)S(6)} %div.7, s32[]{:T(128)S(6)} %select_n.118, s32[16]{0:T(128)S(1)} %get-tuple-element.247, f32[16]{0:T(128)S(1)} %get-tuple-element.246, pred[]{:T(512)S(6)} %lt.122, f32[16]{0:T(128)S(1)} %bitcast.47), kind=kLoop, calls=%fused_computation.14.clone.1 | loop fusion | flops 2162688 | bytes 1441993 | tf_op jit(solution)/shard_map/while/body/eval_jaxpr/mul | solution.py:22
  105.1 1.1 copy.85
  112.1 9.6 %fusion.31 = (f32[16,1,11264]{2,0,1:T(8,128)S(1)}, f32[16,1,11264]{2,0,1:T(8,128)S(1)}) fusion(f32[]{:T(128)S(6)} %div.7, s32[]{:T(128)S(6)} %select_n.118, s32[16]{0:T(128)S(1)} %get-tuple-element.247, f32[16]{0:T(128)S(1)} %get-tuple-element.246, pred[]{:T(512)S(6)} %lt.122, f32[16]{0:T(128)S(1)} %bitcast.47), kind=kLoop, calls=%fused_computation.14.clone.1 | loop fusion | flops 2162688 | bytes 1441993 | tf_op jit(solution)/shard_map/while/body/eval_jaxpr/mul | solution.py:22
  121.8 1.1 copy.85
  128.9 9.6 %fusion.31 = (f32[16,1,11264]{2,0,1:T(8,128)S(1)}, f32[16,1,11264]{2,0,1:T(8,128)S(1)}) fusion(f32[]{:T(128)S(6)} %div.7, s32[]{:T(128)S(6)} %select_n.118, s32[16]{0:T(128)S(1)} %get-tuple-element.247, f32[16]{0:T(128)S(1)} %get-tuple-element.246, pred[]{:T(512)S(6)} %lt.122, f32[16]{0:T(128)S(1)} %bitcast.47), kind=kLoop, calls=%fused_computation.14.clone.1 | loop fusion | flops 2162688 | bytes 1441993 | tf_op jit(solution)/shard_map/while/body/eval_jaxpr/mul | solution.py:22
  138.5 1.1 copy.85
  145.6 9.6 %fusion.31 = (f32[16,1,11264]{2,0,1:T(8,128)S(1)}, f32[16,1,11264]{2,0,1:T(8,128)S(1)}) fusion(f32[]{:T(128)S(6)} %div.7, s32[]{:T(128)S(6)} %select_n.118, s32[16]{0:T(128)S(1)} %get-tuple-element.247, f32[16]{0:T(128)S(1)} %get-tuple-element.246, pred[]{:T(512)S(6)} %lt.122, f32[16]{0:T(128)S(1)} %bitcast.47), kind=kLoop, calls=%fused_computation.14.clone.1 | loop fusion | flops 2162688 | bytes 1441993 | tf_op jit(solution)/shard_map/while/body/eval_jaxpr/mul | solution.py:22
  155.3 1.1 copy.85
  159.5 35.7 %copy.71 = f32[8,3,2,11264]{0,2,1,3:T(2,128)} copy(f32[8,3,2,11264]{3,2,1,0:T(2,128)} %get-tuple-element.78) | data formatting | bytes 4325376 | tf_op jit(solution)/shard_map/while | solution.py:32
  195.2 73.8 %reshape.236 = f32[8,1,67584]{2,1,0:T(1,128)S(1)} reshape(f32[11264,3,2,8]{3,2,1,0:T(2,128)} %bitcast.38) | data formatting | bytes 4325376
  269.0 52.3 %all_to_all.54 = f32[8,1,67584]{2,1,0:T(1,128)} all-to-all(f32[8,1,67584]{2,1,0:T(1,128)S(1)} %reshape.236), channel_id=1, replica_groups=mesh['grp'=4,'wav'=8] {'wav'}, dimensions={0} | all-to-all | bytes 4325376 | tf_op jit(solution)/shard_map/all_to_all | solution.py:61
  321.3 7.4 %reduce.1 = f32[8,67584]{1,0:T(8,128)S(1)} reduce(f32[8,1,67584]{2,1,0:T(1,128)} %all_to_all.54, f32[]{:T(128)} %broadcast.245), dimensions={1}, to_apply=%all_to_all.43.reduce_sub_computation | reduce | bytes 4325380 | tf_op jit(solution)/shard_map/all_to_all | solution.py:61
  328.7 67.0 %reshape.237 = f32[11264,3,2,8]{3,2,1,0:T(2,128)} reshape(f32[8,67584]{1,0:T(8,128)S(1)} %reduce.1) | data formatting | bytes 4325376
  395.6 41.3 %copy.81 = f32[8,3,2,8,1408]{4,0,3,2,1:T(8,128)S(1)} copy(f32[8,3,2,8,1408]{0,2,1,4,3:T(2,128)} %bitcast.39) | data formatting | bytes 4325376 | tf_op jit(solution)/shard_map/all_to_all | solution.py:61
  437.0 1.7 copy.74
  438.7 29.0 %all_to_all.55 = f32[64,3,2,1408]{3,2,1,0:T(2,128)S(1)} all-to-all(f32[64,3,2,1408]{3,2,1,0:T(2,128)S(1)} %copy.74), channel_id=1, replica_groups=mesh['grp'=4,'wav'=8] {'grp'}, dimensions={0} | all-to-all | bytes 4325376 | tf_op jit(solution)/shard_map/all_to_all | solution.py:60
  468.0 2.0 copy.77
  (100 shorter events, 39.1 us)
Async XLA Ops:
  3.2 13.2 %copy-start = (s32[16]{0:T(128)S(1)}, s32[16]{0:T(128)}, u32[]{:S(2)}) copy-start(s32[16]{0:T(128)} %param.9) | copy-start | bytes 196
  3.2 13.2 %copy-start.1 = (s32[32]{0:T(128)S(1)}, s32[32]{0:T(128)}, u32[]{:S(2)}) copy-start(s32[32]{0:T(128)} %param.10) | copy-start | bytes 388
  9.2 13.8 %all-to-all-start = ((f32[8,1,192]{2,1,0:T(1,128)}), f32[8,1,192]{2,1,0:T(1,128)S(1)}, u32[]{:S(2)}, u32[]{:S(2)}) async-start(f32[8,1,192]{2,1,0:T(1,128)} %reshape.234), calls=%async_computation | async-start | bytes 16384 | tf_op jit(solution)/shard_map/all_to_all | solution.py:55
where the time goes:
time: 478 us; the launch traced here: 470 us
  local copies, waits for them, and re-layouts  256 us (54%)
  other arithmetic  94.3 us (20%)
  blocking collectives  81.2 us (17%)
  loops' own time  16.6 us (3%)
  matrix products  8.78 us (2%)
  starting transfers between devices  7.28 us (2%)
  waiting for transfers between devices  5.56 us (1%)
    unnamed x9, local copies, waits for them, and re-layouts  142 us
    mul x8, other arithmetic, one_cycle(): cosine = weight[:, None] * jnp.cos(angles)  76.7 us
    all_to_all x1, blocking collectives, body(): lax.all_to_all(grid_rows, 'wav', split_axis=3, concat_axis=0, tiled=True)  52.3 us
    all_to_all x2, local copies, waits for them, and re-layouts, body(): lax.all_to_all(grid_rows, 'wav', split_axis=3, concat_axis=0, tiled=True)  43 us
    while x1, local copies, waits for them, and re-layouts, synthesis(): return lax.map(one_cycle, (coeffs, lengths))  35.7 us
    all_to_all x1, blocking collectives, body(): lax.all_to_all(lax.all_to_all(grid_rows, 'wav', split_axis=3, concat_axis...  29 us
    another operation x1, loops' own time, synthesis(): return lax.map(one_cycle, (coeffs, lengths))  16.6 us
  transfers between devices with their start and end apart: 1, of which 1 were waited for; matrix products, arithmetic and copies ran while one was open for 0% of the time, Pallas kernels for 0%

commit v1 on v0

v1 whole, which is shorter than its diff:
```python
import functools
import math

import jax
import jax.numpy as jnp
from jax import lax
from jax.experimental import pallas as pl
from jax.experimental.pallas import tpu as pltpu
from jax.sharding import PartitionSpec as P

RMAX = 10256
SLOTS = 8
VMEM_BYTES = 48 * 2**20
MESH = pl.DeviceIdType.MESH


def iota(shape, dim):
    return lax.broadcasted_iota(jnp.int32, shape, dim)


def split(x):
    high = x.astype(jnp.bfloat16)
    return high, (x - high.astype(jnp.float32)).astype(jnp.bfloat16)


def dot(a, b, dims=((1,), (0,))):
    return lax.dot_general(a, b, (dims, ((), ())), preferred_element_type=jnp.float32)


def spread(groups, columns, spec, leg, wave, owner, out, rows, send, send_sem, recv_sem):
    devices = groups * columns
    g, w = lax.axis_index("grp"), lax.axis_index("wav")
    me = g * columns + w
    barrier = pltpu.get_barrier_semaphore()

    def place(step):
        other = lax.rem(me + step, devices)
        return lax.div(other, columns), lax.rem(other, columns)

    @pl.loop(1, devices)
    def _(step):
        pl.semaphore_signal(barrier, inc=1, device_id=place(step), device_id_type=MESH)

    fields, levels, waves, _, degrees = spec.shape
    half = leg.shape[2]
    lanes = send.shape[2]
    lane_row = iota((1, groups * lanes), 1) // SLOTS
    cycle = jnp.zeros((1, groups * lanes), jnp.int32)
    for row in range(2 * half):
        cycle = jnp.where(lane_row == row, owner[row], cycle)
    northern = iota((half, groups * lanes), 0)
    pick = [
        (northern + h * half == cycle).astype(jnp.float32).astype(jnp.bfloat16) for h in range(2)
    ]
    slot = iota((16, groups * lanes), 1) % SLOTS == iota((16, groups * lanes), 0) // 2
    degree = iota((16, degrees), 1)
    placed = []
    for q in range(waves):
        rows[q, 8:16, :] = jnp.zeros((8, degrees), jnp.float32)
        for f in range(fields):
            for l in range(levels):
                at = 2 * (f * levels + l)
                rows[q, at : at + 2, :] = spec[f, l, q]
        number = wave[w * waves + q]
        masked = jnp.where(degree + number < degrees, rows[q], 0.0)
        mirrored = jnp.where(degree % 2 == 0, masked, -masked)
        high, low = split(jnp.concatenate([masked, mirrored], axis=0))
        table_high, table_low = split(leg[q])
        both = dot(jnp.concatenate([high, low], axis=0), table_high)
        fourier = both[:32] + both[32:] + dot(high, table_low)
        total = jnp.zeros((16, groups * lanes), jnp.float32)
        for h in range(2):
            high, low = split(fourier[16 * h : 16 * h + 16])
            moved = dot(jnp.concatenate([high, low], axis=0), pick[h])
            total = total + moved[:16] + moved[16:]
        total = jnp.where(slot, total, 0.0)
        total = total[:8] + total[8:]
        total = total + pltpu.roll(total, 4, 0)
        placed.append(total + pltpu.roll(total, 2, 0))
    message = jnp.where(iota(placed[0].shape, 0) < 2, placed[0], placed[1])
    for to in range(groups):
        send[to] = message[:4, to * lanes : (to + 1) * lanes]
    out[g, w] = send[g]

    pl.semaphore_wait(barrier, devices - 1)

    def copy(step, source):
        to_g, to_w = place(step)
        from_g, from_w = source
        return pltpu.make_async_remote_copy(
            src_ref=send.at[to_g],
            dst_ref=out.at[from_g, from_w],
            send_sem=send_sem.at[to_g, to_w],
            recv_sem=recv_sem.at[from_g, from_w],
            device_id=(to_g, to_w),
            device_id_type=MESH,
        )

    @pl.loop(1, devices)
    def _(step):
        copy(step, (g, w)).start()

    @pl.loop(1, devices)
    def _(step):
        copy(step, place(step)).wait_recv()

    @pl.loop(1, devices)
    def _(step):
        copy(step, (g, w)).wait_send()


def reduced(x, length, inverse):
    turns = jnp.floor(x.astype(jnp.float32) * inverse).astype(jnp.int32)
    left = x - turns * length
    left = jnp.where(left < 0, left + length, left)
    return jnp.where(left >= length, left - length, left)


def cosine(x, length, inverse):
    left = reduced(x, length, inverse)
    left = jnp.where(2 * left > length, left - length, left)
    half = left.astype(jnp.float32) * (inverse * math.pi)
    square = half * half
    series = jnp.full_like(square, 1.0 / math.factorial(13))
    for power in (11, 9, 7, 5, 3, 1):
        sign = -1.0 if power % 4 == 3 else 1.0
        series = series * square + sign / math.factorial(power)
    sine = series * half
    return 1.0 - 2.0 * sine * sine


def synthesis(columns, got, wave, points, owner, out, coeffs, swapped, grid, out_sem):
    groups, lanes = got.shape[0], got.shape[3]
    depth = 4 * columns
    count, fields, level_total, segment = grid.shape
    levels = level_total // groups
    block = fields * level_total
    copies = -(-3 * depth // 128) * 128 // depth
    wide = copies * depth
    tiles = segment // 128
    tile_rows = -(-tiles // 8) * 8
    g, w = lax.axis_index("grp"), lax.axis_index("wav")

    x = jnp.concatenate([got[i].reshape(depth, lanes) for i in range(groups)], axis=1)
    even = iota(x.shape, 0) % 2 == 0
    partner = jnp.where(even, pltpu.roll(x, depth - 1, 0), pltpu.roll(x, 1, 0))
    target = iota((count * block, 1), 0)
    inner = lax.rem(target, block)
    level = lax.rem(inner, level_total)
    target = (
        lax.div(level, levels) * lanes
        + lax.div(target, block) * SLOTS
        + lax.div(inner, level_total) * levels
        + lax.rem(level, levels)
    )
    move = iota((count * block, groups * lanes), 1) == target
    move = move.astype(jnp.float32).astype(jnp.bfloat16)
    for values, ref in ((x, coeffs), (partner, swapped)):
        high, low = split(values)
        ref[...] = dot(move, jnp.concatenate([high] * copies, axis=0), ((1,), (1,))) + dot(
            move, jnp.concatenate([low] * copies, axis=0), ((1,), (1,))
        )

    deep = iota((depth, 128), 0)
    deep_wave = jnp.zeros((depth, 128), jnp.int32)
    across = iota((tile_rows, wide), 1) % depth
    across_wave = jnp.zeros((tile_rows, wide), jnp.int32)
    for q in range(depth // 2):
        deep_wave = jnp.where(deep // 2 == q, wave[q], deep_wave)
        across_wave = jnp.where(across // 2 == q, wave[q], across_wave)
    near = deep_wave * iota((depth, 128), 1)
    far = across_wave * (w * segment + 128 * iota((tile_rows, wide), 0))
    weight = jnp.where(across_wave == 0, 1.0, 2.0)
    rest = (iota((block * tiles, wide), 1) // depth) % 2 == 1
    point = iota((block, 128), 1) + w * segment

    def write(p):
        return pltpu.make_async_copy(grid.at[p], out.at[p], out_sem.at[p])

    @pl.loop(0, count, unroll=4)
    def _(p):
        length = points[lax.rem(owner[g * count + p], points.shape[0])]
        quarter = lax.div(length, 4)
        inverse = 1.0 / jnp.full((1, 128), length, jnp.int32).astype(jnp.float32)
        high, low = split(cosine(near + (deep % 2) * quarter, length, inverse))
        basis = jnp.concatenate([high, high, low, low][:copies], axis=0)
        inverse = jnp.concatenate([inverse] * (wide // 128), axis=1)
        turn = weight * cosine(far, length, inverse)
        cross = weight * cosine(far + (1 + 2 * (across % 2)) * quarter, length, inverse)
        start = pl.multiple_of(p * block, 8)
        own, other = coeffs[pl.ds(start, block), :], swapped[pl.ds(start, block), :]
        turned = jnp.concatenate(
            [own * turn[t : t + 1] + other * cross[t : t + 1] for t in range(tiles)], axis=0
        )
        head = turned.astype(jnp.bfloat16).astype(jnp.float32)
        parts = jnp.where(rest, turned - head, head).astype(jnp.bfloat16)
        values = dot(parts, basis)
        for t in range(tiles):
            kept = jnp.where(point + 128 * t < length, values[t * block : (t + 1) * block], 0.0)
            grid[p, :, :, 128 * t : 128 * (t + 1)] = kept.reshape(fields, level_total, 128)
        write(p).start()

    @pl.loop(0, count)
    def _(p):
        write(p).wait()


def body(groups, columns, spectra, legendre, wave_number, cycle_points, cycle_owner):
    fields, levels, waves, _, degrees = spectra.shape
    half = legendre.shape[2]
    count = 2 * half // groups
    lanes = count * SLOTS
    level_total = levels * groups
    segment = (RMAX + 128 * columns - 1) // (128 * columns) * 128
    vmem, smem = pl.BlockSpec(memory_space=pltpu.VMEM), pl.BlockSpec(memory_space=pltpu.SMEM)
    got = pl.pallas_call(
        functools.partial(spread, groups, columns),
        out_shape=jax.ShapeDtypeStruct((groups, columns, 4, lanes), jnp.float32),
        in_specs=[vmem, vmem, smem, smem],
        out_specs=vmem,
        scratch_shapes=[
            pltpu.VMEM((waves, 16, degrees), jnp.float32),
            pltpu.VMEM((groups, 4, lanes), jnp.float32),
            pltpu.SemaphoreType.DMA((groups, columns)),
            pltpu.SemaphoreType.DMA((groups, columns)),
        ],
        compiler_params=pltpu.CompilerParams(
            collective_id=0, has_side_effects=True, vmem_limit_bytes=VMEM_BYTES
        ),
        name="spread",
    )(spectra, legendre, wave_number, cycle_owner)
    wide = -(-3 * 4 * columns // 128) * 128
    block = fields * level_total
    return pl.pallas_call(
        functools.partial(synthesis, columns),
        out_shape=jax.ShapeDtypeStruct((count, fields, level_total, segment), jnp.float32),
        in_specs=[vmem, smem, smem, smem],
        out_specs=pl.BlockSpec(memory_space=pl.ANY),
        scratch_shapes=[
            pltpu.VMEM((count * block, wide), jnp.float32),
            pltpu.VMEM((count * block, wide), jnp.float32),
            pltpu.VMEM((count, fields, level_total, segment), jnp.float32),
            pltpu.SemaphoreType.DMA((count,)),
        ],
        compiler_params=pltpu.CompilerParams(vmem_limit_bytes=VMEM_BYTES),
        name="synthesis",
    )(got, wave_number, cycle_points, cycle_owner)


def solution(mesh):
    in_specs = (P(None, "grp", "wav", None, None), P("wav", None, None), P(), P(), P())
    out_specs = P("grp", None, None, "wav")
    groups, columns = mesh.shape["grp"], mesh.shape["wav"]
    return jax.shard_map(
        functools.partial(body, groups, columns),
        mesh=mesh,
        in_specs=in_specs,
        out_specs=out_specs,
        check_vma=False,
    )
```

time: 478 us -> 18 us (0.04); the launches traced: 470 us -> 17.8 us
  local copies, waits for them, and re-layouts: 256 us -> 1.86 us
  other arithmetic: 94.3 us -> 0 us
  blocking collectives: 81.2 us -> 0 us
  loops' own time: 16.6 us -> 0 us
  Pallas kernels: 0 us -> 15.9 us
  matrix products: 8.78 us -> 0 us
  starting transfers between devices: 7.28 us -> 0 us
  waiting for transfers between devices: 5.56 us -> 0 us
    unnamed x9, local copies, waits for them, and re-layouts: 142 us -> 1.86 us
    all_to_all x2 -> x0, blocking collectives: 81.2 us -> none  [the longest x1 52.3 us: body(): lax.all_to_all(grid_rows, 'wav', split_axis=3, concat_axis=0, tiled=True)]
    mul x9 -> x0, other arithmetic: 77.8 us -> none  [the longest x8 76.7 us: one_cycle(): cosine = weight[:, None] * jnp.cos(angles)]
    all_to_all x8 -> x0, local copies, waits for them, and re-layouts: 46.3 us -> none  [the longest x2 43 us: body(): lax.all_to_all(grid_rows, 'wav', split_axis=3, concat_axis=0, tiled=True)]
    while x1 -> x0, local copies, waits for them, and re-layouts: 35.7 us -> none  [synthesis(): return lax.map(one_cycle, (coeffs, lengths))]
    another operation x1 -> x0, loops' own time: 16.6 us -> none  [synthesis(): return lax.map(one_cycle, (coeffs, lengths))]
    pallas_call x0 -> x2, Pallas kernels: none -> 15.9 us  [the longest x1 11.9 us: body(): pl.pallas_call(functools.partial(spread, groups, columns), out_shape=jax....]
    another operation x8 -> x0, local copies, waits for them, and re-layouts: 8.91 us -> none  [one_cycle(): jnp.stack([cosine, sine_part], axis=1).reshape(2 * wave_total, points_count)]
  transfers between devices with their start and end apart: 1 -> 0, of which waited for: 1 -> 0; matrix products, arithmetic and copies ran while one was open for 0% -> 0% of each run, Pallas kernels for 0% -> 0%
where the time goes in v1:
time: 18 us; the launch traced here: 17.8 us
  Pallas kernels  15.9 us (88%)
  local copies, waits for them, and re-layouts  1.86 us (10%)
    pallas_call x1, Pallas kernels, body(): pl.pallas_call(functools.partial(spread, groups, columns), out_shape=jax....  11.9 us
    pallas_call x1, Pallas kernels, body(): pl.pallas_call(functools.partial(synthesis, columns), out_shape=jax.Shape...  4.05 us
    unnamed x9, local copies, waits for them, and re-layouts  1.86 us

profile of v1, /device:TPU:0, one launch (start us, length us, event | category | flops | bytes accessed | tf_op | source)
XLA Modules:
  0.0 17.8 jit_solution(3637602664189688535)
XLA Ops:
  0.0 0.0 copy-start.2
  0.0 0.0 copy-start.1
  0.0 0.0 copy-start.3
  0.0 0.0 copy-start
  0.0 1.8 %copy.6.leg = f32[2,2560,32]{2,1,0:T(8,128)S(1)} copy(f32[2,2560,32]{1,2,0:T(8,128)} %param.6) | data formatting | bytes 1310720 | tf_op args[1]
  1.9 0.0 copy-done.2
  1.9 0.0 copy-done.1
  1.9 0.0 copy-done
  1.9 11.9 %spread.1.got = f32[4,8,4,128]{3,2,1,0:T(4,128)S(1)} custom-call(f32[3,2,2,2,2560]{4,3,2,1,0:T(2,128)S(1)} %copy-done, f32[2,2560,32]{2,1,0:T(8,128)S(1)} %copy.6.leg, s32[16]{0:T(128)S(1)} %copy-done.1, s32[64]{0:T(128)S(1)} %copy-done.2), custom_call_target="tpu_custom_call" | custom-call | tf_op jit(solution)/shard_map/spread/pallas_call | solution.py:216
  13.8 0.0 copy-done.3
  13.8 4.1 %synthesis.1 = f32[16,3,8,1408]{3,2,1,0:T(8,128)} custom-call(f32[4,8,4,128]{3,2,1,0:T(4,128)S(1)} %spread.1.got, s32[16]{0:T(128)S(1)} %copy-done.1, s32[32]{0:T(128)S(1)} %copy-done.3, s32[64]{0:T(128)S(1)} %copy-done.2), custom_call_target="tpu_custom_call" | custom-call | tf_op jit(solution)/shard_map/synthesis/pallas_call | solution.py:234
Async XLA Ops:
  0.0 1.9 %copy-start.2 = (s32[64]{0:T(128)S(1)}, s32[64]{0:T(128)}, u32[]{:S(2)}) copy-start(s32[64]{0:T(128)} %owner.3) | copy-start | bytes 772
  0.0 1.9 %copy-start.1 = (s32[16]{0:T(128)S(1)}, s32[16]{0:T(128)}, u32[]{:S(2)}) copy-start(s32[16]{0:T(128)} %wave.3) | copy-start | bytes 196
  0.0 13.8 %copy-start.3 = (s32[32]{0:T(128)S(1)}, s32[32]{0:T(128)}, u32[]{:S(2)}) copy-start(s32[32]{0:T(128)} %points.1) | copy-start | bytes 388
  0.0 1.9 %copy-start = (f32[3,2,2,2,2560]{4,3,2,1,0:T(2,128)S(1)}, f32[3,2,2,2,2560]{4,3,2,1,0:T(2,128)}, u32[]{:S(2)}) copy-start(f32[3,2,2,2,2560]{4,3,2,1,0:T(2,128)} %spec.1) | copy-start | bytes 737284

commit v2 on v1

v2 whole, which is shorter than its diff:
```python
import functools
import math

import jax
import jax.numpy as jnp
from jax import lax
from jax.experimental import pallas as pl
from jax.experimental.pallas import tpu as pltpu
from jax.sharding import PartitionSpec as P

RMAX = 10256
SLOTS = 8
VMEM_BYTES = 48 * 2**20
MESH = pl.DeviceIdType.MESH


def iota(shape, dim):
    return lax.broadcasted_iota(jnp.int32, shape, dim)


def split(x):
    high = x.astype(jnp.bfloat16)
    return high, (x - high.astype(jnp.float32)).astype(jnp.bfloat16)


def dot(a, b, dims=((1,), (0,))):
    return lax.dot_general(a, b, (dims, ((), ())), preferred_element_type=jnp.float32)


def reduced(x, length, inverse):
    turns = jnp.floor(x.astype(jnp.float32) * inverse).astype(jnp.int32)
    left = x - turns * length
    left = jnp.where(left < 0, left + length, left)
    return jnp.where(left >= length, left - length, left)


def cosine(x, length, inverse):
    left = reduced(x, length, inverse)
    left = jnp.where(2 * left > length, left - length, left)
    half = left.astype(jnp.float32) * (inverse * math.pi)
    square = half * half
    series = jnp.full_like(square, 1.0 / math.factorial(13))
    for power in (11, 9, 7, 5, 3, 1):
        sign = -1.0 if power % 4 == 3 else 1.0
        series = series * square + sign / math.factorial(power)
    sine = series * half
    return 1.0 - 2.0 * sine * sine


def tables(groups, columns, level_total, segment, wave, points, owner, move, basis, turn, cross):
    count, wide = basis.shape[:2]
    lanes, depth, levels = count * SLOTS, 4 * columns, level_total // groups
    block, copies, tile_rows = move.shape[0] // count, wide // depth, turn.shape[1]
    g, w = lax.axis_index("grp"), lax.axis_index("wav")
    target = iota((count * block, 1), 0)
    inner = lax.rem(target, block)
    level = lax.rem(inner, level_total)
    target = (
        lax.div(level, levels) * lanes
        + lax.div(target, block) * SLOTS
        + lax.div(inner, level_total) * levels
        + lax.rem(level, levels)
    )
    chosen = iota((count * block, groups * lanes), 1) == target
    move[...] = chosen.astype(jnp.float32).astype(jnp.bfloat16)
    deep = iota((depth, 128), 0)
    deep_wave = jnp.zeros((depth, 128), jnp.int32)
    across = iota((tile_rows, wide), 1) % depth
    across_wave = jnp.zeros((tile_rows, wide), jnp.int32)
    for q in range(depth // 2):
        deep_wave = jnp.where(deep // 2 == q, wave[q], deep_wave)
        across_wave = jnp.where(across // 2 == q, wave[q], across_wave)
    near = deep_wave * iota((depth, 128), 1)
    far = across_wave * (w * segment + 128 * iota((tile_rows, wide), 0))
    weight = jnp.where(across_wave == 0, 1.0, 2.0)

    @pl.loop(0, count, unroll=4)
    def _(p):
        length = points[lax.rem(owner[g * count + p], points.shape[0])]
        quarter = lax.div(length, 4)
        inverse = 1.0 / jnp.full((1, 128), length, jnp.int32).astype(jnp.float32)
        high, low = split(cosine(near + (deep % 2) * quarter, length, inverse))
        basis[p] = jnp.concatenate([high, high, low, low][:copies], axis=0)
        inverse = jnp.concatenate([inverse] * (wide // 128), axis=1)
        turn[p] = weight * cosine(far, length, inverse)
        cross[p] = weight * cosine(far + (1 + 2 * (across % 2)) * quarter, length, inverse)


def spread(
    groups, columns, segment, spec_in, leg_in, wave, points, owner, out, move, basis, turn, cross, spec,
    leg, rows, send, send_sem, recv_sem, in_sem,
):
    devices = groups * columns
    g, w = lax.axis_index("grp"), lax.axis_index("wav")
    me = g * columns + w
    barrier = pltpu.get_barrier_semaphore()
    loads = [
        pltpu.make_async_copy(spec_in, spec, in_sem.at[0]),
        pltpu.make_async_copy(leg_in, leg, in_sem.at[1]),
    ]
    for load in loads:
        load.start()

    def place(step):
        other = lax.rem(me + step, devices)
        return lax.div(other, columns), lax.rem(other, columns)

    @pl.loop(1, devices)
    def _(step):
        pl.semaphore_signal(barrier, inc=1, device_id=place(step), device_id_type=MESH)

    fields, levels, waves, _, degrees = spec.shape
    half = leg.shape[1]
    lanes = send.shape[2]
    lane_row = iota((1, groups * lanes), 1) // SLOTS
    cycle = jnp.zeros((1, groups * lanes), jnp.int32)
    for row in range(2 * half):
        cycle = jnp.where(lane_row == row, owner[row], cycle)
    northern = iota((half, groups * lanes), 0)
    pick = [
        (northern + h * half == cycle).astype(jnp.float32).astype(jnp.bfloat16) for h in range(2)
    ]
    slot = iota((16, groups * lanes), 1) % SLOTS == iota((16, groups * lanes), 0) // 2
    degree = iota((16, degrees), 1)
    placed = []
    for load in loads:
        load.wait()
    for q in range(waves):
        rows[q, 8:16, :] = jnp.zeros((8, degrees), jnp.float32)
        for f in range(fields):
            for l in range(levels):
                at = 2 * (f * levels + l)
                rows[q, at : at + 2, :] = spec[f, l, q]
        number = wave[w * waves + q]
        masked = jnp.where(degree + number < degrees, rows[q], 0.0)
        mirrored = jnp.where(degree % 2 == 0, masked, -masked)
        high, low = split(jnp.concatenate([masked, mirrored], axis=0))
        table_high, table_low = split(leg[q])
        both = dot(jnp.concatenate([high, low], axis=0), table_high, ((1,), (1,)))
        fourier = both[:32] + both[32:] + dot(high, table_low, ((1,), (1,)))
        total = jnp.zeros((16, groups * lanes), jnp.float32)
        for h in range(2):
            high, low = split(fourier[16 * h : 16 * h + 16])
            moved = dot(jnp.concatenate([high, low], axis=0), pick[h])
            total = total + moved[:16] + moved[16:]
        total = jnp.where(slot, total, 0.0)
        total = total[:8] + total[8:]
        total = total + pltpu.roll(total, 4, 0)
        placed.append(total + pltpu.roll(total, 2, 0))
    message = jnp.where(iota(placed[0].shape, 0) < 2, placed[0], placed[1])
    for to in range(groups):
        send[to] = message[:4, to * lanes : (to + 1) * lanes]
    out[g, w] = send[g]

    pl.semaphore_wait(barrier, devices - 1)

    def copy(step, source):
        to_g, to_w = place(step)
        from_g, from_w = source
        return pltpu.make_async_remote_copy(
            src_ref=send.at[to_g],
            dst_ref=out.at[from_g, from_w],
            send_sem=send_sem.at[to_g, to_w],
            recv_sem=recv_sem.at[from_g, from_w],
            device_id=(to_g, to_w),
            device_id_type=MESH,
        )

    @pl.loop(1, devices)
    def _(step):
        copy(step, (g, w)).start()

    tables(groups, columns, levels * groups, segment, wave, points, owner, move, basis, turn, cross)

    @pl.loop(1, devices)
    def _(step):
        copy(step, place(step)).wait_recv()

    @pl.loop(1, devices)
    def _(step):
        copy(step, (g, w)).wait_send()


def synthesis(columns, got, move, basis, turn, cross, points, owner, out, coeffs, swapped, grid, out_sem):
    groups, lanes = got.shape[0], got.shape[3]
    depth = 4 * columns
    count, fields, level_total, segment = grid.shape
    levels = level_total // groups
    block = fields * level_total
    copies = -(-3 * depth // 128) * 128 // depth
    wide = copies * depth
    tiles = segment // 128
    g, w = lax.axis_index("grp"), lax.axis_index("wav")

    x = jnp.concatenate([got[i].reshape(depth, lanes) for i in range(groups)], axis=1)
    even = iota(x.shape, 0) % 2 == 0
    partner = jnp.where(even, pltpu.roll(x, depth - 1, 0), pltpu.roll(x, 1, 0))
    for values, ref in ((x, coeffs), (partner, swapped)):
        high, low = split(values)
        ref[...] = dot(move[...], jnp.concatenate([high] * copies, axis=0), ((1,), (1,))) + dot(
            move[...], jnp.concatenate([low] * copies, axis=0), ((1,), (1,))
        )

    rest = (iota((block * tiles, wide), 1) // depth) % 2 == 1
    point = iota((block, 128), 1) + w * segment

    def write(p):
        return pltpu.make_async_copy(grid.at[p], out.at[p], out_sem.at[p])

    @pl.loop(0, count, unroll=4)
    def _(p):
        length = points[lax.rem(owner[g * count + p], points.shape[0])]
        start = pl.multiple_of(p * block, 8)
        own, other = coeffs[pl.ds(start, block), :], swapped[pl.ds(start, block), :]
        turned = jnp.concatenate(
            [own * turn[p, t : t + 1] + other * cross[p, t : t + 1] for t in range(tiles)], axis=0
        )
        head = turned.astype(jnp.bfloat16).astype(jnp.float32)
        parts = jnp.where(rest, turned - head, head).astype(jnp.bfloat16)
        values = dot(parts, basis[p])
        for t in range(tiles):
            kept = jnp.where(point + 128 * t < length, values[t * block : (t + 1) * block], 0.0)
            grid[p, :, :, 128 * t : 128 * (t + 1)] = kept.reshape(fields, level_total, 128)
        write(p).start()

    @pl.loop(0, count)
    def _(p):
        write(p).wait()


def body(groups, columns, spectra, legendre, wave_number, cycle_points, cycle_owner):
    fields, levels, waves, _, degrees = spectra.shape
    half = legendre.shape[2]
    count = 2 * half // groups
    lanes = count * SLOTS
    level_total = levels * groups
    segment = (RMAX + 128 * columns - 1) // (128 * columns) * 128
    vmem, smem = pl.BlockSpec(memory_space=pltpu.VMEM), pl.BlockSpec(memory_space=pltpu.SMEM)
    wide = -(-3 * 4 * columns // 128) * 128
    block = fields * level_total
    angles = jax.ShapeDtypeStruct((count, -(-segment // 1024) * 8, wide), jnp.float32)
    got, *angles = pl.pallas_call(
        functools.partial(spread, groups, columns, segment),
        out_shape=(
            jax.ShapeDtypeStruct((groups, columns, 4, lanes), jnp.float32),
            jax.ShapeDtypeStruct((count * block, groups * lanes), jnp.bfloat16),
            jax.ShapeDtypeStruct((count, wide, 128), jnp.bfloat16),
            angles,
            angles,
        ),
        in_specs=[pl.BlockSpec(memory_space=pltpu.HBM)] * 2 + [smem] * 3,
        out_specs=(vmem,) * 5,
        scratch_shapes=[
            pltpu.VMEM(spectra.shape, jnp.float32),
            pltpu.VMEM((waves, half, degrees), jnp.float32),
            pltpu.VMEM((waves, 16, degrees), jnp.float32),
            pltpu.VMEM((groups, 4, lanes), jnp.float32),
            pltpu.SemaphoreType.DMA((groups, columns)),
            pltpu.SemaphoreType.DMA((groups, columns)),
            pltpu.SemaphoreType.DMA((2,)),
        ],
        compiler_params=pltpu.CompilerParams(
            collective_id=0, has_side_effects=True, vmem_limit_bytes=VMEM_BYTES
        ),
        name="spread",
    )(spectra, jnp.swapaxes(legendre, 1, 2), wave_number, cycle_points, cycle_owner)
    return pl.pallas_call(
        functools.partial(synthesis, columns),
        out_shape=jax.ShapeDtypeStruct((count, fields, level_total, segment), jnp.float32),
        in_specs=[vmem] * 5 + [smem] * 2,
        out_specs=pl.BlockSpec(memory_space=pl.ANY),
        scratch_shapes=[
            pltpu.VMEM((count * block, wide), jnp.float32),
            pltpu.VMEM((count * block, wide), jnp.float32),
            pltpu.VMEM((count, fields, level_total, segment), jnp.float32),
            pltpu.SemaphoreType.DMA((count,)),
        ],
        compiler_params=pltpu.CompilerParams(vmem_limit_bytes=VMEM_BYTES),
        name="synthesis",
    )(got, *angles, cycle_points, cycle_owner)


def solution(mesh):
    in_specs = (P(None, "grp", "wav", None, None), P("wav", None, None), P(), P(), P())
    out_specs = P("grp", None, None, "wav")
    groups, columns = mesh.shape["grp"], mesh.shape["wav"]
    return jax.shard_map(
        functools.partial(body, groups, columns),
        mesh=mesh,
        in_specs=in_specs,
        out_specs=out_specs,
        check_vma=False,
    )
```

time: 18 us -> 19.7 us (1.094)
  local copies, waits for them, and re-layouts: 1.86 us -> 3.99 us
  Pallas kernels: 15.9 us -> 15.5 us
    unnamed x9 -> x10, local copies, waits for them, and re-layouts: 1.86 us -> 3.99 us
    pallas_call x1, Pallas kernels: 4.05 us -> 3.22 us  [body(): pl.pallas_call(functools.partial(synthesis, columns), out_shape=jax.Shape...]
    pallas_call x1, Pallas kernels: 11.9 us -> 12.3 us  [body(): pl.pallas_call(functools.partial(spread, groups, columns, segment), out_s...]
where the time goes in v2:
time: 19.7 us; the launch traced here: 19.5 us
  Pallas kernels  15.5 us (79%)
  local copies, waits for them, and re-layouts  3.99 us (20%)
    pallas_call x1, Pallas kernels, body(): pl.pallas_call(functools.partial(spread, groups, columns, segment), out_s...  12.3 us
    unnamed x10, local copies, waits for them, and re-layouts  3.99 us
    pallas_call x1, Pallas kernels, body(): pl.pallas_call(functools.partial(synthesis, columns), out_shape=jax.Shape...  3.22 us

profile of v2, /device:TPU:0, one launch (start us, length us, event | category | flops | bytes accessed | tf_op | source)
XLA Modules:
  0.0 19.5 jit_solution(7450967315039312929)
XLA Ops:
  0.0 0.0 copy-start
  0.0 1.1 %copy-done = f32[2,2560,32]{1,2,0:T(8,128)S(1)} copy-done((f32[2,2560,32]{1,2,0:T(8,128)S(1)}, f32[2,2560,32]{1,2,0:T(8,128)}, u32[]{:S(2)}) %copy-start) | copy-done | bytes 655384
  1.1 0.0 copy-start.1
  1.1 0.9 %copy-done.1 = f32[3,2,2,2,2560]{4,3,2,1,0:T(2,128)S(1)} copy-done((f32[3,2,2,2,2560]{4,3,2,1,0:T(2,128)S(1)}, f32[3,2,2,2,2560]{4,3,2,1,0:T(2,128)}, u32[]{:S(2)}) %copy-start.1) | copy-done | bytes 245784
  2.0 0.0 copy-start.2
  2.0 0.7 %copy-done.2 = s32[32]{0:T(128)S(1)} copy-done((s32[32]{0:T(128)S(1)}, s32[32]{0:T(128)}, u32[]{:S(2)}) %copy-start.2) | copy-done | bytes 152
  2.7 0.0 copy-start.3
  2.7 0.7 %copy-done.3 = s32[64]{0:T(128)S(1)} copy-done((s32[64]{0:T(128)S(1)}, s32[64]{0:T(128)}, u32[]{:S(2)}) %copy-start.3) | copy-done | bytes 280
  3.3 0.0 copy-start.4
  3.3 0.7 %copy-done.4 = s32[16]{0:T(128)S(1)} copy-done((s32[16]{0:T(128)S(1)}, s32[16]{0:T(128)}, u32[]{:S(2)}) %copy-start.4) | copy-done | bytes 88
  4.0 12.3 %spread.1 = (f32[4,8,4,128]{3,2,1,0:T(4,128)S(1)}, bf16[384,512]{1,0:T(8,128)(2,1)S(1)}, bf16[16,128,128]{2,1,0:T(8,128)(2,1)S(1)}, f32[16,16,128]{2,1,0:T(8,128)S(1)}, f32[16,16,128]{2,1,0:T(8,128)S(1)}) custom-call(f32[3,2,2,2,2560]{4,3,2,1,0:T(2,128)S(1)} %copy-done.1, f32[2,32,2560]{2,1,0:T(8,128)S(1)} %bitcast.1, s32[16]{0:T(128)S(1)} %copy-done.4, ...), custom_call_target="tpu_custom_call" | custom-call | tf_op jit(solution)/shard_map/spread/pallas_call | solution.py:242
  16.3 3.2 %synthesis.1 = f32[16,3,8,1408]{3,2,1,0:T(8,128)} custom-call(f32[4,8,4,128]{3,2,1,0:T(4,128)S(1)} %get-tuple-element.10.got, bf16[384,512]{1,0:T(8,128)(2,1)S(1)} %get-tuple-element.11.move, bf16[16,128,128]{2,1,0:T(8,128)(2,1)S(1)} %get-tuple-element.12.basis, f32[16,16,128]{2,1,0:T(8,128)S(1)} %get-tuple-element.13.turn, ...), custom_call_target="tpu_custom_call" | custom-call | tf_op jit(solution)/shard_map/synthesis/pallas_call | solution.py:267
Async XLA Ops:
  0.0 1.1 %copy-start = (f32[2,2560,32]{1,2,0:T(8,128)S(1)}, f32[2,2560,32]{1,2,0:T(8,128)}, u32[]{:S(2)}) copy-start(f32[2,2560,32]{1,2,0:T(8,128)} %param.6) | copy-start | bytes 1966084
  1.1 0.9 %copy-start.1 = (f32[3,2,2,2,2560]{4,3,2,1,0:T(2,128)S(1)}, f32[3,2,2,2,2560]{4,3,2,1,0:T(2,128)}, u32[]{:S(2)}) copy-start(f32[3,2,2,2,2560]{4,3,2,1,0:T(2,128)} %spec_in.1) | copy-start | bytes 737284
  2.0 0.7 %copy-start.2 = (s32[32]{0:T(128)S(1)}, s32[32]{0:T(128)}, u32[]{:S(2)}) copy-start(s32[32]{0:T(128)} %points.3) | copy-start | bytes 388
  2.7 0.7 %copy-start.3 = (s32[64]{0:T(128)S(1)}, s32[64]{0:T(128)}, u32[]{:S(2)}) copy-start(s32[64]{0:T(128)} %owner.3) | copy-start | bytes 772
  3.3 0.7 %copy-start.4 = (s32[16]{0:T(128)S(1)}, s32[16]{0:T(128)}, u32[]{:S(2)}) copy-start(s32[16]{0:T(128)} %wave.1) | copy-start | bytes 196

commit v3 on v1

--- a/solution.py
+++ b/solution.py
@@ -10,7 +10,7 @@
 
 RMAX = 10256
 SLOTS = 8
-VMEM_BYTES = 48 * 2**20
+VMEM_BYTES = 65000 * 2**10
 MESH = pl.DeviceIdType.MESH
 
 
@@ -27,11 +27,17 @@
     return lax.dot_general(a, b, (dims, ((), ())), preferred_element_type=jnp.float32)
 
 
-def spread(groups, columns, spec, leg, wave, owner, out, rows, send, send_sem, recv_sem):
+def spread(groups, columns, spec_in, leg_in, wave, owner, out, spec, leg, rows, send, send_sem, recv_sem, in_sem):
     devices = groups * columns
     g, w = lax.axis_index("grp"), lax.axis_index("wav")
     me = g * columns + w
     barrier = pltpu.get_barrier_semaphore()
+    loads = [
+        pltpu.make_async_copy(spec_in, spec, in_sem.at[0]),
+        pltpu.make_async_copy(leg_in, leg, in_sem.at[1]),
+    ]
+    for load in loads:
+        load.start()
 
     def place(step):
         other = lax.rem(me + step, devices)
@@ -42,7 +48,7 @@
         pl.semaphore_signal(barrier, inc=1, device_id=place(step), device_id_type=MESH)
 
     fields, levels, waves, _, degrees = spec.shape
-    half = leg.shape[2]
+    half = leg.shape[1]
     lanes = send.shape[2]
     lane_row = iota((1, groups * lanes), 1) // SLOTS
     cycle = jnp.zeros((1, groups * lanes), jnp.int32)
@@ -55,6 +61,8 @@
     slot = iota((16, groups * lanes), 1) % SLOTS == iota((16, groups * lanes), 0) // 2
     degree = iota((16, degrees), 1)
     placed = []
+    for load in loads:
+        load.wait()
     for q in range(waves):
         rows[q, 8:16, :] = jnp.zeros((8, degrees), jnp.float32)
         for f in range(fields):
@@ -66,8 +74,8 @@
         mirrored = jnp.where(degree % 2 == 0, masked, -masked)
         high, low = split(jnp.concatenate([masked, mirrored], axis=0))
         table_high, table_low = split(leg[q])
-        both = dot(jnp.concatenate([high, low], axis=0), table_high)
-        fourier = both[:32] + both[32:] + dot(high, table_low)
+        both = dot(jnp.concatenate([high, low], axis=0), table_high, ((1,), (1,)))
+        fourier = both[:32] + both[32:] + dot(high, table_low, ((1,), (1,)))
         total = jnp.zeros((16, groups * lanes), jnp.float32)
         for h in range(2):
             high, low = split(fourier[16 * h : 16 * h + 16])
@@ -216,19 +224,22 @@
     got = pl.pallas_call(
         functools.partial(spread, groups, columns),
         out_shape=jax.ShapeDtypeStruct((groups, columns, 4, lanes), jnp.float32),
-        in_specs=[vmem, vmem, smem, smem],
+        in_specs=[pl.BlockSpec(memory_space=pltpu.HBM)] * 2 + [smem, smem],
         out_specs=vmem,
         scratch_shapes=[
+            pltpu.VMEM(spectra.shape, jnp.float32),
+            pltpu.VMEM((waves, half, degrees), jnp.float32),
             pltpu.VMEM((waves, 16, degrees), jnp.float32),
             pltpu.VMEM((groups, 4, lanes), jnp.float32),
             pltpu.SemaphoreType.DMA((groups, columns)),
             pltpu.SemaphoreType.DMA((groups, columns)),
+            pltpu.SemaphoreType.DMA((2,)),
         ],
         compiler_params=pltpu.CompilerParams(
             collective_id=0, has_side_effects=True, vmem_limit_bytes=VMEM_BYTES
         ),
         name="spread",
-    )(spectra, legendre, wave_number, cycle_owner)
+    )(spectra, jnp.swapaxes(legendre, 1, 2), wave_number, cycle_owner)
     wide = -(-3 * 4 * columns // 128) * 128
     block = fields * level_total
     return pl.pallas_call(

time: 18 us -> 17.6 us (0.978)
  local copies, waits for them, and re-layouts: 1.86 us -> 0 us
  Pallas kernels: 15.9 us -> 17.4 us
    unnamed x9 -> x0, local copies, waits for them, and re-layouts: 1.86 us -> none
    pallas_call x1, Pallas kernels: 11.9 us -> 13 us  [body(): pl.pallas_call(functools.partial(spread, groups, columns), out_shape=jax....]
    pallas_call x1, Pallas kernels: 4.05 us -> 4.35 us  [body(): pl.pallas_call(functools.partial(synthesis, columns), out_shape=jax.Shape...]
where the time goes in v3:
time: 17.6 us; the launch traced here: 17.4 us
  Pallas kernels  17.4 us (99%)
    pallas_call x1, Pallas kernels, body(): pl.pallas_call(functools.partial(spread, groups, columns), out_shape=jax....  13 us
    pallas_call x1, Pallas kernels, body(): pl.pallas_call(functools.partial(synthesis, columns), out_shape=jax.Shape...  4.35 us

profile of v3, /device:TPU:0, one launch (start us, length us, event | category | flops | bytes accessed | tf_op | source)
XLA Modules:
  0.0 17.4 jit_solution(6748867074450994450)
XLA Ops:
  0.0 13.0 %spread.1.got = f32[4,8,4,128]{3,2,1,0:T(4,128)} custom-call(f32[3,2,2,2,2560]{4,3,2,1,0:T(2,128)} %spec_in.1, f32[2,32,2560]{2,1,0:T(8,128)} %bitcast.1, s32[16]{0:T(128)} %wave.3, s32[64]{0:T(128)} %owner.3), custom_call_target="tpu_custom_call" | custom-call | tf_op jit(solution)/shard_map/spread/pallas_call | solution.py:224
  13.0 4.4 %synthesis.1 = f32[16,3,8,1408]{3,2,1,0:T(8,128)} custom-call(f32[4,8,4,128]{3,2,1,0:T(4,128)} %spread.1.got, s32[16]{0:T(128)} %wave.3, s32[32]{0:T(128)} %points.1, s32[64]{0:T(128)} %owner.3), custom_call_target="tpu_custom_call" | custom-call | tf_op jit(solution)/shard_map/synthesis/pallas_call | solution.py:245

commit v4 on v3

--- a/solution.py
+++ b/solution.py
@@ -30,7 +30,6 @@
 def spread(groups, columns, spec_in, leg_in, wave, owner, out, spec, leg, rows, send, send_sem, recv_sem, in_sem):
     devices = groups * columns
     g, w = lax.axis_index("grp"), lax.axis_index("wav")
-    me = g * columns + w
     barrier = pltpu.get_barrier_semaphore()
     loads = [
         pltpu.make_async_copy(spec_in, spec, in_sem.at[0]),
@@ -39,13 +38,14 @@
     for load in loads:
         load.start()
 
-    def place(step):
-        other = lax.rem(me + step, devices)
-        return lax.div(other, columns), lax.rem(other, columns)
-
-    @pl.loop(1, devices)
-    def _(step):
-        pl.semaphore_signal(barrier, inc=1, device_id=place(step), device_id_type=MESH)
+    def each(act):
+        for over in range(groups):
+
+            @pl.loop(1 if over == 0 else 0, columns, unroll=columns if columns <= 8 and over else 1)
+            def _(along):
+                act(lax.rem(g + over, groups), lax.rem(w + along, columns))
+
+    each(lambda *to: pl.semaphore_signal(barrier, inc=1, device_id=to, device_id_type=MESH))
 
     fields, levels, waves, _, degrees = spec.shape
     half = leg.shape[1]
@@ -92,29 +92,19 @@
 
     pl.semaphore_wait(barrier, devices - 1)
 
-    def copy(step, source):
-        to_g, to_w = place(step)
-        from_g, from_w = source
+    def copy(to, source):
         return pltpu.make_async_remote_copy(
-            src_ref=send.at[to_g],
-            dst_ref=out.at[from_g, from_w],
-            send_sem=send_sem.at[to_g, to_w],
-            recv_sem=recv_sem.at[from_g, from_w],
-            device_id=(to_g, to_w),
+            src_ref=send.at[to[0]],
+            dst_ref=out.at[source[0], source[1]],
+            send_sem=send_sem.at[to[0], to[1]],
+            recv_sem=recv_sem.at[source[0], source[1]],
+            device_id=to,
             device_id_type=MESH,
         )
 
-    @pl.loop(1, devices)
-    def _(step):
-        copy(step, (g, w)).start()
-
-    @pl.loop(1, devices)
-    def _(step):
-        copy(step, place(step)).wait_recv()
-
-    @pl.loop(1, devices)
-    def _(step):
-        copy(step, (g, w)).wait_send()
+    each(lambda *to: copy(to, (g, w)).start())
+    each(lambda *source: copy(source, source).wait_recv())
+    each(lambda *to: copy(to, (g, w)).wait_send())
 
 
 def reduced(x, length, inverse):
@@ -185,7 +175,7 @@
     def write(p):
         return pltpu.make_async_copy(grid.at[p], out.at[p], out_sem.at[p])
 
-    @pl.loop(0, count, unroll=4)
+    @pl.loop(0, count, unroll=8)
     def _(p):
         length = points[lax.rem(owner[g * count + p], points.shape[0])]
         quarter = lax.div(length, 4)

time: 17.6 us -> 17.3 us (0.983)
  Pallas kernels: 17.4 us -> 17.1 us
    pallas_call x1, Pallas kernels: 4.35 us -> 4.15 us  [body(): pl.pallas_call(functools.partial(synthesis, columns), out_shape=jax.Shape...]
where the time goes in v4:
time: 17.3 us; the launch traced here: 17.1 us
  Pallas kernels  17.1 us (99%)
    pallas_call x1, Pallas kernels, body(): pl.pallas_call(functools.partial(spread, groups, columns), out_shape=jax....  12.9 us
    pallas_call x1, Pallas kernels, body(): pl.pallas_call(functools.partial(synthesis, columns), out_shape=jax.Shape...  4.15 us

profile of v4, /device:TPU:0, one launch (start us, length us, event | category | flops | bytes accessed | tf_op | source)
XLA Modules:
  0.0 17.1 jit_solution(10418802110512833755)
XLA Ops:
  0.0 12.9 %spread.1.got = f32[4,8,4,128]{3,2,1,0:T(4,128)} custom-call(f32[3,2,2,2,2560]{4,3,2,1,0:T(2,128)} %spec_in.1, f32[2,32,2560]{2,1,0:T(8,128)} %bitcast.1, s32[16]{0:T(128)} %wave.3, s32[64]{0:T(128)} %owner.3), custom_call_target="tpu_custom_call" | custom-call | tf_op jit(solution)/shard_map/spread/pallas_call | solution.py:214
  12.9 4.1 %synthesis.1 = f32[16,3,8,1408]{3,2,1,0:T(8,128)} custom-call(f32[4,8,4,128]{3,2,1,0:T(4,128)} %spread.1.got, s32[16]{0:T(128)} %wave.3, s32[32]{0:T(128)} %points.1, s32[64]{0:T(128)} %owner.3), custom_call_target="tpu_custom_call" | custom-call | tf_op jit(solution)/shard_map/synthesis/pallas_call | solution.py:235

commit v5 on v4

--- a/solution.py
+++ b/solution.py
@@ -41,7 +41,7 @@
     def each(act):
         for over in range(groups):
 
-            @pl.loop(1 if over == 0 else 0, columns, unroll=columns if columns <= 8 and over else 1)
+            @pl.loop(1 if over == 0 else 0, columns, unroll=columns - (over == 0) if columns <= 8 else 1)
             def _(along):
                 act(lax.rem(g + over, groups), lax.rem(w + along, columns))
 
@@ -175,7 +175,7 @@
     def write(p):
         return pltpu.make_async_copy(grid.at[p], out.at[p], out_sem.at[p])
 
-    @pl.loop(0, count, unroll=8)
+    @pl.loop(0, count, unroll=16)
     def _(p):
         length = points[lax.rem(owner[g * count + p], points.shape[0])]
         quarter = lax.div(length, 4)

time: 17.3 us -> 16.9 us (0.977)
  Pallas kernels: 17.1 us -> 16.7 us
    pallas_call x1, Pallas kernels: 4.15 us -> 3.8 us  [body(): pl.pallas_call(functools.partial(synthesis, columns), out_shape=jax.Shape...]
where the time goes in v5:
time: 16.9 us; the launch traced here: 16.7 us
  Pallas kernels  16.7 us (99%)
    pallas_call x1, Pallas kernels, body(): pl.pallas_call(functools.partial(spread, groups, columns), out_shape=jax....  12.9 us
    pallas_call x1, Pallas kernels, body(): pl.pallas_call(functools.partial(synthesis, columns), out_shape=jax.Shape...  3.8 us

profile of v5, /device:TPU:0, one launch (start us, length us, event | category | flops | bytes accessed | tf_op | source)
XLA Modules:
  0.0 16.7 jit_solution(17511350314316131260)
XLA Ops:
  0.0 12.9 %spread.1.got = f32[4,8,4,128]{3,2,1,0:T(4,128)} custom-call(f32[3,2,2,2,2560]{4,3,2,1,0:T(2,128)} %spec_in.1, f32[2,32,2560]{2,1,0:T(8,128)} %bitcast.1, s32[16]{0:T(128)} %wave.3, s32[64]{0:T(128)} %owner.3), custom_call_target="tpu_custom_call" | custom-call | tf_op jit(solution)/shard_map/spread/pallas_call | solution.py:214
  12.9 3.8 %synthesis.1 = f32[16,3,8,1408]{3,2,1,0:T(8,128)} custom-call(f32[4,8,4,128]{3,2,1,0:T(4,128)} %spread.1.got, s32[16]{0:T(128)} %wave.3, s32[32]{0:T(128)} %points.1, s32[64]{0:T(128)} %owner.3), custom_call_target="tpu_custom_call" | custom-call | tf_op jit(solution)/shard_map/synthesis/pallas_call | solution.py:235
